TPU v7x, 32 devices: a whole 2x2x4 slice. The times are simulated.
32 devices in a mesh: dp: 8 (over z, x), mp: 4 (over y, core).
Axes of the slice: x: 2, y: 2, z: 4, core: 2. Of those that a mesh axis runs over, the one named last changes fastest.
Arguments:
- features: bfloat16 [8, 320, 128, 128], P('dp', 'mp'), may hold values from -6 to 6
- w_out: bfloat16 [320, 36], P('mp'), may hold values from -0.109375 to 0.109375
- noisy_latent: float32 [8, 4, 128, 128], P('dp', None, 'mp'), may hold values from -6 to 6
- timestep: int32 [8], P('dp'), may hold values from 100 to 699
- w_in: bfloat16 [9, 512, 4], replicated, may hold values from -1 to 1
- b_in: float32 [512], replicated, may hold values from -3 to 3
- w_mid: bfloat16 [9, 512, 512], replicated, may hold values from -0.09375 to 0.09375
- b_mid: float32 [512], replicated, may hold values from -3 to 3
- reward_head: float32 [512], replicated, may hold values from -6 to 6
Outputs:
- feature_grads: bfloat16 [8, 320, 128, 128], P('dp', 'mp')
- weight_grad: float32 [320, 36], P('mp')
All inputs are finite; a program needn't handle non-finite values.
Results may differ from a plain program's by a relative error of at most 0.012.
Values may be sent and summed in bfloat16 or wider, within the bound.
No kernel may reach another device: no remote copies, remote signals or barrier semaphores. Data moves between devices by JAX's collectives and lax.ppermute only.
A program may use at most 192 MiB of HBM per device.

v0:
```python
import jax
import jax.numpy as jnp
from jax import lax
from jax.sharding import PartitionSpec as P


def with_halo(shard, sides, width):
    for axis, dim in sides:
        devices, length = (lax.axis_size(axis), shard.shape[dim])
        up = [(i, (i + 1) % devices) for i in range(devices - 1)]
        down = [(j, i) for i, j in up]
        last = lax.slice_in_dim(shard, length - width, length, axis=dim)
        first = lax.slice_in_dim(shard, 0, width, axis=dim)
        before = lax.ppermute(last, axis, up)
        after = lax.ppermute(first, axis, down)
        shard = jnp.concatenate([before, shard, after], axis=dim)
    return shard


def noise_levels(timestep):
    betas = jnp.linspace(0.00085**0.5, 0.012**0.5, 1000, dtype=jnp.float32) ** 2
    table = jnp.cumprod(1.0 - betas)
    hits = jnp.arange(1000, dtype=jnp.int32)[None, :] == timestep[:, None]
    return jnp.sum(jnp.where(hits, table[None, :], jnp.float32(0.0)), axis=1)


def pad_both(source):
    return jnp.pad(source, ((0, 0), (1, 1), (1, 1)))


def pad_cols(source):
    return jnp.pad(source, ((0, 0), (0, 0), (1, 1)))


def slope(value):
    sig = jax.nn.sigmoid(value)
    return sig * (1.0 + value * (1.0 - sig))


def conv_taps(padded, kernel, out_rows, out_cols):
    summed = jnp.zeros((kernel.shape[1], out_rows * out_cols), jnp.float32)
    for tap in range(9):
        tap_row, tap_col = (tap // 3, tap % 3)
        window = padded[:, tap_row : tap_row + out_rows, tap_col : tap_col + out_cols].reshape(
            padded.shape[0], -1
        )
        summed = summed + jnp.dot(kernel[tap], window, preferred_element_type=jnp.float32)
    return summed.reshape(kernel.shape[1], out_rows, out_cols)


def conv_back(padded, kernel, out_rows, out_cols):
    summed = jnp.zeros((kernel.shape[2], out_rows * out_cols), jnp.float32)
    for tap in range(9):
        tap_row, tap_col = (tap // 3, tap % 3)
        window = padded[
            :, 2 - tap_row : 2 - tap_row + out_rows, 2 - tap_col : 2 - tap_col + out_cols
        ].reshape(padded.shape[0], -1)
        summed = summed + jnp.dot(kernel[tap].T, window, preferred_element_type=jnp.float32)
    return summed.reshape(kernel.shape[2], out_rows, out_cols)


def weight_taps(padded, noise_grad, out_rows, out_cols):
    flat = noise_grad.reshape(noise_grad.shape[0], -1)
    parts = []
    for tap in range(9):
        tap_row, tap_col = (tap // 3, tap % 3)
        window = padded[:, tap_row : tap_row + out_rows, tap_col : tap_col + out_cols].reshape(
            padded.shape[0], -1
        )
        parts.append(jnp.dot(window, flat.T, preferred_element_type=jnp.float32))
    return jnp.concatenate(parts, axis=1)


def body(features, w_out, noisy_latent, timestep, w_in, b_in, w_mid, b_mid, reward_head):
    images, channels, crop_rows, col_count = features.shape
    lat_chans = noisy_latent.shape[1]
    row_count = noisy_latent.shape[2]
    eps_kernel = jnp.transpose(w_out.reshape(channels, 9, lat_chans), (1, 2, 0))
    partial_value = jnp.stack([conv_taps(pad_both(features[0]), eps_kernel, crop_rows, col_count)])
    eps = lax.psum_scatter(partial_value, "mp", scatter_dimension=2, tiled=True)
    noise_level = noise_levels(timestep)
    root_a = jnp.sqrt(noise_level)[:, None, None, None]
    root_b = jnp.sqrt(1.0 - noise_level)[:, None, None, None]
    latent = ((noisy_latent - root_b * eps) / root_a).astype(jnp.bfloat16)
    bias_in = b_in[:, None, None]
    bias_mid = b_mid[:, None, None]
    latent_ext = with_halo(latent, (("mp", 2),), 1)
    hidden_pre = jnp.stack(
        [conv_taps(pad_cols(latent_ext[0]), w_in, row_count, col_count) + bias_in]
    )
    hidden_act = jax.nn.silu(hidden_pre).astype(jnp.bfloat16)
    hidden_ext = with_halo(hidden_act, (("mp", 2),), 1)
    mixed_pre = jnp.stack(
        [conv_taps(pad_cols(hidden_ext[0]), w_mid, row_count, col_count) + bias_mid]
    )
    mixed_grad = (reward_head[None, :, None, None] * slope(mixed_pre)).astype(jnp.bfloat16)
    mixed_ext = with_halo(mixed_grad, (("mp", 2),), 1)
    act_grad = jnp.stack([conv_back(pad_cols(mixed_ext[0]), w_mid, row_count, col_count)])
    hidden_grad = (act_grad * slope(hidden_pre)).astype(jnp.bfloat16)
    grad_ext = with_halo(hidden_grad, (("mp", 2),), 1)
    latent_grad = jnp.stack([conv_back(pad_cols(grad_ext[0]), w_in, row_count, col_count)])
    noise_grad = (-(root_b / root_a) * latent_grad).astype(jnp.bfloat16)
    full_grads = lax.all_gather(noise_grad, "mp", axis=2, tiled=True)
    feature_grads = jnp.stack(
        [conv_back(pad_both(full_grads[0]), eps_kernel, crop_rows, col_count)]
    ).astype(jnp.bfloat16)
    weight_local = weight_taps(pad_both(features[0]), full_grads[0], crop_rows, col_count)
    weight_grad = lax.psum(weight_local, "dp") / (crop_rows * col_count)
    return (feature_grads, weight_grad)


def solution(mesh):
    in_specs = (
        P("dp", "mp", None, None),
        P("mp", None),
        P("dp", None, "mp", None),
        P("dp"),
        P(),
        P(),
        P(),
        P(),
        P(),
    )
    out_specs = (P("dp", "mp", None, None), P("mp", None))
    return jax.shard_map(body, mesh=mesh, in_specs=in_specs, out_specs=out_specs, check_vma=False)
```

profile of v0, /device:TPU:0, one launch (start us, length us, event | category | flops | bytes accessed | tf_op | source)
XLA Modules:
  0.0 478.6 jit_solution(4126128048617846616)
XLA Ops:
  7.9 17.6 %pad_slice_fusion = (bf16[80,128,128]{2,1,0:T(8,128)(2,1)S(1)}, bf16[80,128,128]{2,1,0:T(8,128)(2,1)S(1)}, bf16[80,128,128]{2,1,0:T(8,128)(2,1)S(1)}, bf16[80,12...) fusion(bf16[80,128,128]{2,1,0:T(8,128)(2,1)} %bitcast.405), kind=kLoop, calls=%fused_computation.22 | loop fusion | bytes 23592960 | tf_op jit(solution)/shard_map/slice | solution.py:44
  43.6 19.7 %reduce-scatter.2.cloned.1.call-done = f32[1,4,32,128]{3,2,1,0:T(8,128)} async-done(((f32[1,4,128,128]{3,2,1,0:T(8,128)}), f32[1,4,32,128]{3,2,1,0:T(8,128)}) %reduce-scatter.2.cloned.1.call-update) | async-done | bytes 65552 | tf_op jit(solution)/shard_map/reduce_scatter | solution.py:80
  83.0 4.6 fusion.152
  87.6 4.6 fusion.149
  106.0 25.1 %add_add_fusion.2 = f32[4096,512]{1,0:T(8,128)} fusion(f32[4096,512]{1,0:T(8,128)} %fusion.149, f32[4096,512]{1,0:T(8,128)} %fusion.152, f32[4096,512]{1,0:T(8,128)} %fusion.155, f32[4096,512]{1,0:T(8,128)} %fusion.158, f32[4096,512]{1,0:T(8,128)} %fusion.161, f32[4096,512]{1,0:T(8,128)} %fusion.164, f32[4096,512]{1,0:T(8,128)} %fusion.170, ...), kind=kOutput, calls=%fused_computation.32 | convolution fusion | flops 33554432 | bytes 75534336 | tf_op jit(solution)/shard_map/dot_general | solution.py:47
  143.8 15.2 %pad_slice_fusion.20 = (bf16[512,32,128]{0,2,1:T(8,128)(2,1)}, bf16[512,32,128]{0,2,1:T(8,128)(2,1)}, bf16[512,32,128]{0,2,1:T(8,128)(2,1)}, bf16[512,32,128]{0,...) fusion(bf16[512,34,128]{0,2,1:T(8,128)(2,1)S(1)} %maximum_bitca, ...), kind=kLoop, calls=%fused_computation.62 | loop fusion | bytes 54788096 | tf_op jit(solution)/shard_map/slice | solution.py:44
  159.0 8.0 %fusion.87 = f32[4096,512]{1,0:T(8,128)} fusion(bf16[512,4096]{0,1:T(8,128)(2,1)} %bitcast.426, bf16[9,512,512]{2,1,0:T(8,128)(2,1)S(1)} %bitcast.409), kind=kOutput, calls=%fused_computation.141 | convolution fusion | flops 2147483648 | bytes 13107200 | tf_op jit(solution)/shard_map/dot_general | solution.py:47
  167.0 5.8 %fusion.83 = f32[4096,512]{1,0:T(8,128)} fusion(bf16[512,4096]{0,1:T(8,128)(2,1)S(1)} %bitcast.424, bf16[9,512,512]{2,1,0:T(8,128)(2,1)S(1)} %bitcast.409), kind=kOutput, calls=%fused_computation.137 | convolution fusion | flops 2147483648 | bytes 13107200 | tf_op jit(solution)/shard_map/dot_general | solution.py:47
  172.9 5.9 %fusion.75 = f32[4096,512]{1,0:T(8,128)} fusion(bf16[512,4096]{0,1:T(8,128)(2,1)S(1)} %bitcast.422, bf16[9,512,512]{2,1,0:T(8,128)(2,1)S(1)} %bitcast.409), kind=kOutput, calls=%fused_computation.129 | convolution fusion | flops 2147483648 | bytes 13107200 | tf_op jit(solution)/shard_map/dot_general | solution.py:47
  178.8 5.8 %fusion.71 = f32[4096,512]{1,0:T(8,128)} fusion(bf16[512,4096]{0,1:T(8,128)(2,1)S(1)} %bitcast.420, bf16[9,512,512]{2,1,0:T(8,128)(2,1)S(1)} %bitcast.409), kind=kOutput, calls=%fused_computation.125 | convolution fusion | flops 2147483648 | bytes 13107200 | tf_op jit(solution)/shard_map/dot_general | solution.py:47
  184.6 5.8 %fusion.67 = f32[4096,512]{1,0:T(8,128)} fusion(bf16[512,4096]{0,1:T(8,128)(2,1)S(1)} %bitcast.418, bf16[9,512,512]{2,1,0:T(8,128)(2,1)S(1)} %bitcast.409), kind=kOutput, calls=%fused_computation.121 | convolution fusion | flops 2147483648 | bytes 13107200 | tf_op jit(solution)/shard_map/dot_general | solution.py:47
  190.4 6.2 %fusion.79 = f32[4096,512]{1,0:T(8,128)} fusion(bf16[512,4096]{0,1:T(8,128)(2,1)S(1)} %bitcast.416, bf16[9,512,512]{2,1,0:T(8,128)(2,1)S(1)} %bitcast.409), kind=kOutput, calls=%fused_computation.133 | convolution fusion | flops 2147483648 | bytes 13107200 | tf_op jit(solution)/shard_map/dot_general | solution.py:47
  196.7 5.8 %fusion.91 = f32[4096,512]{1,0:T(8,128)} fusion(bf16[512,4096]{0,1:T(8,128)(2,1)S(1)} %bitcast.414, bf16[9,512,512]{2,1,0:T(8,128)(2,1)S(1)} %bitcast.409), kind=kOutput, calls=%fused_computation.145 | convolution fusion | flops 2147483648 | bytes 13107200 | tf_op jit(solution)/shard_map/dot_general | solution.py:47
  202.5 5.8 %fusion.95 = f32[4096,512]{1,0:T(8,128)} fusion(bf16[512,4096]{0,1:T(8,128)(2,1)S(1)} %bitcast.412, bf16[9,512,512]{2,1,0:T(8,128)(2,1)S(1)} %bitcast.409), kind=kOutput, calls=%fused_computation.149 | convolution fusion | flops 2147483648 | bytes 13107200 | tf_op jit(solution)/shard_map/dot_general | solution.py:47
  208.3 26.8 %add_add_fusion.1 = f32[4096,512]{1,0:T(8,128)} fusion(f32[4096,512]{1,0:T(8,128)} %fusion.67, f32[4096,512]{1,0:T(8,128)} %fusion.71, f32[4096,512]{1,0:T(8,128)} %fusion.75, f32[4096,512]{1,0:T(8,128)} %fusion.79, f32[4096,512]{1,0:T(8,128)} %fusion.83, f32[4096,512]{1,0:T(8,128)} %fusion.87, f32[4096,512]{1,0:T(8,128)} %fusion.95, ...), kind=kOutput, calls=%fused_computation.31 | convolution fusion | flops 2164260864 | bytes 80216064 | tf_op jit(solution)/shard_map/dot_general | solution.py:47
  235.1 5.2 %multiply_convert_fusion.1 = bf16[1,512,32,128]{1,3,2,0:T(8,128)(2,1)S(1)} fusion(f32[1,512,32,128]{1,3,2,0:T(8,128)} %bitcast.395, f32[512]{0:T(512)S(1)} %copy-done.43, f32[512]{0:T(512)S(1)} %copy-done.44), kind=kLoop, calls=%fused_computation.34 | loop fusion | flops 20971520 | bytes 12587008 | tf_op jit(solution)/shard_map/convert_element_type | solution.py:96
  240.4 5.0 %collective-permute-start.4 = (bf16[1,512,1,128]{1,3,2,0:T(8,128)(2,1)S(1)}, bf16[1,512,1,128]{1,3,2,0:T(8,128)(2,1)S(1)}, u32[]{:S(2)}, u32[]{:S(2)}) collective-permute-start(bf16[1,512,1,128]{1,3,2,0:T(8,128)(2,1)S(1)} %get-tuple-element.31), channel_id=1, source_target_pairs={{0,1},{1,2},{2,3},{4,5},{5,6},{6,7},{8,9},{9,10},{10,11},{12,13},{... | collective-permute-start | bytes 393224 | tf_op jit(solution)/shard_map/ppermute | solution.py:14
  249.2 17.2 %pad_slice_fusion.14 = (bf16[512,32,128]{0,2,1:T(8,128)(2,1)}, bf16[512,32,128]{0,2,1:T(8,128)(2,1)}, bf16[512,32,128]{0,2,1:T(8,128)(2,1)}, bf16[512,32,128]{0,...) fusion(bf16[512,34,128]{0,2,1:T(8,128)(2,1)S(1)} %maximum_bitca, ...), kind=kLoop, calls=%fused_computation.56 | loop fusion | bytes 54788096 | tf_op jit(solution)/shard_map/slice | solution.py:55
  266.5 8.0 %fusion.85 = f32[4096,512]{1,0:T(8,128)} fusion(bf16[512,4096]{0,1:T(8,128)(2,1)} %bitcast.427, bf16[9,512,512]{2,1,0:T(8,128)(2,1)S(1)} %bitcast.411), kind=kOutput, calls=%fused_computation.139 | convolution fusion | flops 2147483648 | bytes 13107200 | tf_op jit(solution)/shard_map/dot_general | solution.py:58
  274.5 5.7 %fusion.81 = f32[4096,512]{1,0:T(8,128)} fusion(bf16[512,4096]{0,1:T(8,128)(2,1)S(1)} %bitcast.425, bf16[9,512,512]{2,1,0:T(8,128)(2,1)S(1)} %bitcast.411), kind=kOutput, calls=%fused_computation.135 | convolution fusion | flops 2147483648 | bytes 13107200 | tf_op jit(solution)/shard_map/dot_general | solution.py:58
  280.3 5.7 %fusion.73 = f32[4096,512]{1,0:T(8,128)} fusion(bf16[512,4096]{0,1:T(8,128)(2,1)S(1)} %bitcast.423, bf16[9,512,512]{2,1,0:T(8,128)(2,1)S(1)} %bitcast.411), kind=kOutput, calls=%fused_computation.127 | convolution fusion | flops 2147483648 | bytes 13107200 | tf_op jit(solution)/shard_map/dot_general | solution.py:58
  286.0 5.7 %fusion.69 = f32[4096,512]{1,0:T(8,128)} fusion(bf16[512,4096]{0,1:T(8,128)(2,1)S(1)} %bitcast.421, bf16[9,512,512]{2,1,0:T(8,128)(2,1)S(1)} %bitcast.411), kind=kOutput, calls=%fused_computation.123 | convolution fusion | flops 2147483648 | bytes 13107200 | tf_op jit(solution)/shard_map/dot_general | solution.py:58
  291.7 5.7 %fusion.65 = f32[4096,512]{1,0:T(8,128)} fusion(bf16[512,4096]{0,1:T(8,128)(2,1)S(1)} %bitcast.419, bf16[9,512,512]{2,1,0:T(8,128)(2,1)S(1)} %bitcast.411), kind=kOutput, calls=%fused_computation.119 | convolution fusion | flops 2147483648 | bytes 13107200 | tf_op jit(solution)/shard_map/dot_general | solution.py:58
  297.4 5.7 %fusion.77 = f32[4096,512]{1,0:T(8,128)} fusion(bf16[512,4096]{0,1:T(8,128)(2,1)S(1)} %bitcast.417, bf16[9,512,512]{2,1,0:T(8,128)(2,1)S(1)} %bitcast.411), kind=kOutput, calls=%fused_computation.131 | convolution fusion | flops 2147483648 | bytes 13107200 | tf_op jit(solution)/shard_map/dot_general | solution.py:58
  303.1 6.1 %fusion.89 = f32[4096,512]{1,0:T(8,128)} fusion(bf16[512,4096]{0,1:T(8,128)(2,1)S(1)} %bitcast.415, bf16[9,512,512]{2,1,0:T(8,128)(2,1)S(1)} %bitcast.411), kind=kOutput, calls=%fused_computation.143 | convolution fusion | flops 2147483648 | bytes 13107200 | tf_op jit(solution)/shard_map/dot_general | solution.py:58
  309.2 5.7 %fusion.93 = f32[4096,512]{1,0:T(8,128)} fusion(bf16[512,4096]{0,1:T(8,128)(2,1)S(1)} %bitcast.413, bf16[9,512,512]{2,1,0:T(8,128)(2,1)S(1)} %bitcast.411), kind=kOutput, calls=%fused_computation.147 | convolution fusion | flops 2147483648 | bytes 13107200 | tf_op jit(solution)/shard_map/dot_general | solution.py:58
  314.9 26.7 %add_add_fusion = f32[4096,512]{1,0:T(8,128)} fusion(f32[4096,512]{1,0:T(8,128)} %fusion.65, f32[4096,512]{1,0:T(8,128)} %fusion.69, f32[4096,512]{1,0:T(8,128)} %fusion.73, f32[4096,512]{1,0:T(8,128)} %fusion.77, f32[4096,512]{1,0:T(8,128)} %fusion.81, f32[4096,512]{1,0:T(8,128)} %fusion.85, f32[4096,512]{1,0:T(8,128)} %fusion.93, ...), kind=kOutput, calls=%fused_computation.30 | convolution fusion | flops 2164260864 | bytes 80216064 | tf_op jit(solution)/shard_map/dot_general | solution.py:58
  341.6 7.4 %multiply_convert_fusion = bf16[1,512,32,128]{1,3,2,0:T(8,128)(2,1)S(1)} fusion(f32[1,512,32,128]{1,3,2,0:T(8,128)} %bitcast.394, f32[1,512,32,128]{1,3,2,0:T(8,128)} %bitcast.393, f32[512]{0:T(512)S(1)} %copy-done.42), kind=kLoop, calls=%fused_computation.33 | loop fusion | flops 20971520 | bytes 20973568 | tf_op jit(solution)/shard_map/convert_element_type | solution.py:99
  351.0 4.9 %collective-permute-start.6 = (bf16[1,512,1,128]{1,3,2,0:T(8,128)(2,1)S(1)}, bf16[1,512,1,128]{1,3,2,0:T(8,128)(2,1)S(1)}, u32[]{:S(2)}, u32[]{:S(2)}) collective-permute-start(bf16[1,512,1,128]{1,3,2,0:T(8,128)(2,1)S(1)} %get-tuple-element.29), channel_id=1, source_target_pairs={{0,1},{1,2},{2,3},{4,5},{5,6},{6,7},{8,9},{9,10},{10,11},{12,13},{... | collective-permute-start | bytes 393224 | tf_op jit(solution)/shard_map/ppermute | solution.py:14
  361.8 14.9 %fusion.225 = (bf16[512,32,128]{0,2,1:T(8,128)(2,1)S(1)}, bf16[512,32,128]{0,2,1:T(8,128)(2,1)}, bf16[512,32,128]{0,2,1:T(8,128)(2,1)}, bf16[512,32,128]{0,2,1:T...) fusion(bf16[512,34,128]{0,2,1:T(8,128)(2,1)S(1)} %maximum_bitca, ...), kind=kLoop, calls=%fused_computation.309 | loop fusion | bytes 54788096 | tf_op jit(solution)/shard_map/slice | solution.py:55
  393.2 7.5 %all_gather.3 = bf16[1,4,128,128]{3,1,0,2:T(4,128)(2,1)S(1)} all-gather(bf16[1,4,32,128]{3,1,0,2:T(4,128)(2,1)S(1)} %fusion.59), channel_id=1, replica_groups=mesh['dp'=8,'mp'=4] {'mp'}, dimensions={2}, use_global_device_ids=true | all-gather | bytes 163840 | tf_op jit(solution)/shard_map/all_gather | solution.py:103
  422.7 37.7 %psum.7 = f32[80,36]{0,1:T(8,128)S(1)} all-reduce(f32[80,36]{0,1:T(8,128)S(1)} %concatenate.24), channel_id=1, replica_groups=mesh['dp'=8,'mp'=4] {'dp'}, use_global_device_ids=true, to_apply=%region_4.5 | all-reduce | flops 2880 | bytes 23040 | tf_op jit(solution)/shard_map/psum | solution.py:108
  (183 shorter events, 123.9 us)
Async XLA Ops:
  7.2 56.2 %reduce-scatter.2.cloned.1.call-start = ((), (), s32[]{:S(2)}) async-start(), calls=%async_computation.1 | async-start | bytes 327680 | tf_op jit(solution)/shard_map/reduce_scatter | solution.py:80
  7.9 30.3 %copy-start.40 = (bf16[80,9,4]{0,2,1:T(4,128)(2,1)}, bf16[80,9,4]{0,2,1:T(4,128)(2,1)S(1)}, u32[]{:S(2)}) copy-start(bf16[80,9,4]{0,2,1:T(4,128)(2,1)S(1)} %reshape.395) | copy-start | bytes 17284
  25.6 9.2 %copy-start.25 = (bf16[80,128,128]{2,1,0:T(8,128)(2,1)}, bf16[80,128,128]{2,1,0:T(8,128)(2,1)S(1)}, u32[]{:S(2)}) copy-start(bf16[80,128,128]{2,1,0:T(8,128)(2,1)S(1)} %get-tuple-element.40) | copy-start | bytes 7864324
  25.6 10.7 %copy-start.23 = (bf16[80,128,128]{2,1,0:T(8,128)(2,1)}, bf16[80,128,128]{2,1,0:T(8,128)(2,1)S(1)}, u32[]{:S(2)}) copy-start(bf16[80,128,128]{2,1,0:T(8,128)(2,1)S(1)} %get-tuple-element.41) | copy-start | bytes 7864324
  25.6 12.6 %copy-start.21 = (bf16[80,128,128]{2,1,0:T(8,128)(2,1)}, bf16[80,128,128]{2,1,0:T(8,128)(2,1)S(1)}, u32[]{:S(2)}) copy-start(bf16[80,128,128]{2,1,0:T(8,128)(2,1)S(1)} %get-tuple-element.35) | copy-start | bytes 7864324
  25.6 14.1 %copy-start.29 = (bf16[80,128,128]{2,1,0:T(8,128)(2,1)}, bf16[80,128,128]{2,1,0:T(8,128)(2,1)S(1)}, u32[]{:S(2)}) copy-start(bf16[80,128,128]{2,1,0:T(8,128)(2,1)S(1)} %get-tuple-element.38) | copy-start | bytes 7864324
  25.6 14.1 %copy-start.31 = (bf16[80,128,128]{2,1,0:T(8,128)(2,1)}, bf16[80,128,128]{2,1,0:T(8,128)(2,1)S(1)}, u32[]{:S(2)}) copy-start(bf16[80,128,128]{2,1,0:T(8,128)(2,1)S(1)} %get-tuple-element.37) | copy-start | bytes 7864324
  25.6 14.1 %copy-start.33 = (bf16[80,128,128]{2,1,0:T(8,128)(2,1)}, bf16[80,128,128]{2,1,0:T(8,128)(2,1)S(1)}, u32[]{:S(2)}) copy-start(bf16[80,128,128]{2,1,0:T(8,128)(2,1)S(1)} %get-tuple-element.36) | copy-start | bytes 7864324
  25.6 14.1 %copy-start.35 = (bf16[80,128,128]{2,1,0:T(8,128)(2,1)}, bf16[80,128,128]{2,1,0:T(8,128)(2,1)S(1)}, u32[]{:S(2)}) copy-start(bf16[80,128,128]{2,1,0:T(8,128)(2,1)S(1)} %get-tuple-element.42) | copy-start | bytes 7864324
  36.3 27.1 %copy-start.39 = (f32[1,4,32,128]{3,2,1,0:T(8,128)S(1)}, f32[1,4,32,128]{3,2,1,0:T(8,128)}, u32[]{:S(2)}) copy-start(f32[1,4,32,128]{3,2,1,0:T(8,128)} %param.11) | copy-start | bytes 196612
  36.3 33.0 %copy-start.37 = (bf16[9,512,4]{1,2,0:T(4,128)(2,1)S(1)}, bf16[9,512,4]{1,2,0:T(4,128)(2,1)}, u32[]{:S(2)}) copy-start(bf16[9,512,4]{1,2,0:T(4,128)(2,1)} %param.13) | copy-start | bytes 110596
  64.2 3.0 collective-permute-start
  65.9 3.2 collective-permute-start.1
  106.0 25.1 %copy-start.42 = (f32[512]{0:T(512)S(1)}, f32[512]{0:T(512)}, u32[]{:S(2)}) copy-start(f32[512]{0:T(512)} %param.14) | copy-start | bytes 6148
  135.7 5.6 %collective-permute-start.2 = (bf16[1,512,1,128]{1,3,2,0:T(8,128)(2,1)S(1)}, bf16[1,512,1,128]{1,3,2,0:T(8,128)(2,1)S(1)}, u32[]{:S(2)}, u32[]{:S(2)}) collective-permute-start(bf16[1,512,1,128]{1,3,2,0:T(8,128)(2,1)S(1)} %get-tuple-element.33), channel_id=1, source_target_pairs={{0,1},{1,2},{2,3},{4,5},{5,6},{6,7},{8,9},{9,10},{10,11},{12,13},{... | collective-permute-start | bytes 393224 | tf_op jit(solution)/shard_map/ppermute | solution.py:14
  139.9 3.2 collective-permute-start.3
  143.2 15.8 %slice-start = ((s8[4718592]{0:T(1024)(128)(4,1)}), s8[4194304]{0:T(1024)(128)(4,1)S(1)}, s32[]{:S(2)}) async-start(s8[4718592]{0:T(1024)(128)(4,1)} %bitcast.408), calls=%async_computation.2 | async-start | bytes 8388608
  143.8 15.2 %slice-start.1 = ((s8[4718592]{0:T(1024)(128)(4,1)}), s8[524288]{0:T(1024)(128)(4,1)S(1)}, s32[]{:S(2)}) async-start(s8[4718592]{0:T(1024)(128)(4,1)} %bitcast.408), calls=%async_computation.3 | async-start | bytes 1048576
  159.0 8.0 %copy-start.19 = (bf16[512,32,128]{0,2,1:T(8,128)(2,1)S(1)}, bf16[512,32,128]{0,2,1:T(8,128)(2,1)}, u32[]{:S(2)}) copy-start(bf16[512,32,128]{0,2,1:T(8,128)(2,1)} %get-tuple-element.22) | copy-start | bytes 12582916
  208.3 26.8 %copy-start.43 = (f32[512]{0:T(512)S(1)}, f32[512]{0:T(512)}, u32[]{:S(2)}) copy-start(f32[512]{0:T(512)} %param.16) | copy-start | bytes 6148
  208.3 26.8 %copy-start.44 = (f32[512]{0:T(512)S(1)}, f32[512]{0:T(512)}, u32[]{:S(2)}) copy-start(f32[512]{0:T(512)} %param.17) | copy-start | bytes 6148
  240.4 6.3 %collective-permute-start.4 = (bf16[1,512,1,128]{1,3,2,0:T(8,128)(2,1)S(1)}, bf16[1,512,1,128]{1,3,2,0:T(8,128)(2,1)S(1)}, u32[]{:S(2)}, u32[]{:S(2)}) collective-permute-start(bf16[1,512,1,128]{1,3,2,0:T(8,128)(2,1)S(1)} %get-tuple-element.31), channel_id=1, source_target_pairs={{0,1},{1,2},{2,3},{4,5},{5,6},{6,7},{8,9},{9,10},{10,11},{12,13},{... | collective-permute-start | bytes 393224 | tf_op jit(solution)/shard_map/ppermute | solution.py:14
  245.4 3.2 collective-permute-start.5
  248.6 17.9 %slice-start.2 = ((s8[4718592]{0:T(1024)(128)(4,1)}), s8[4194304]{0:T(1024)(128)(4,1)S(1)}, s32[]{:S(2)}) async-start(s8[4718592]{0:T(1024)(128)(4,1)} %bitcast.410), calls=%async_computation.4 | async-start | bytes 8388608
  249.2 17.3 %slice-start.3 = ((s8[4718592]{0:T(1024)(128)(4,1)}), s8[524288]{0:T(1024)(128)(4,1)S(1)}, s32[]{:S(2)}) async-start(s8[4718592]{0:T(1024)(128)(4,1)} %bitcast.410), calls=%async_computation.5 | async-start | bytes 1048576
  351.0 6.3 %collective-permute-start.6 = (bf16[1,512,1,128]{1,3,2,0:T(8,128)(2,1)S(1)}, bf16[1,512,1,128]{1,3,2,0:T(8,128)(2,1)S(1)}, u32[]{:S(2)}, u32[]{:S(2)}) collective-permute-start(bf16[1,512,1,128]{1,3,2,0:T(8,128)(2,1)S(1)} %get-tuple-element.29), channel_id=1, source_target_pairs={{0,1},{1,2},{2,3},{4,5},{5,6},{6,7},{8,9},{9,10},{10,11},{12,13},{... | collective-permute-start | bytes 393224 | tf_op jit(solution)/shard_map/ppermute | solution.py:14
  356.0 3.2 collective-permute-start.7
  361.8 14.9 %copy-start.38 = (bf16[9,512,4]{1,2,0:T(4,128)(2,1)S(1)}, bf16[9,512,4]{1,2,0:T(4,128)(2,1)}, u32[]{:S(2)}) copy-start(bf16[9,512,4]{1,2,0:T(4,128)(2,1)} %param.13) | copy-start | bytes 110596
  392.0 8.7 %copy-start.36 = (bf16[80,128,128]{2,1,0:T(8,128)(2,1)S(1)}, bf16[80,128,128]{2,1,0:T(8,128)(2,1)}, u32[]{:S(2)}) copy-start(bf16[80,128,128]{2,1,0:T(8,128)(2,1)} %copy-done.35) | copy-start | bytes 7864324
  392.0 11.1 %copy-start.34 = (bf16[80,128,128]{2,1,0:T(8,128)(2,1)S(1)}, bf16[80,128,128]{2,1,0:T(8,128)(2,1)}, u32[]{:S(2)}) copy-start(bf16[80,128,128]{2,1,0:T(8,128)(2,1)} %copy-done.33) | copy-start | bytes 7864324
  393.2 12.3 %copy-start.32 = (bf16[80,128,128]{2,1,0:T(8,128)(2,1)S(1)}, bf16[80,128,128]{2,1,0:T(8,128)(2,1)}, u32[]{:S(2)}) copy-start(bf16[80,128,128]{2,1,0:T(8,128)(2,1)} %copy-done.31) | copy-start | bytes 7864324
  415.4 45.7 %copy-start.41 = (bf16[80,9,4]{0,2,1:T(4,128)(2,1)S(1)}, bf16[80,9,4]{0,2,1:T(4,128)(2,1)}, u32[]{:S(2)}) copy-start(bf16[80,9,4]{0,2,1:T(4,128)(2,1)} %copy-done.40) | copy-start | bytes 17284
  (26 other events, 139.5 us)
Sparse Core Ops, SparseCore 0:
  40.6 22.7 reduce-scatter.1
where the time goes:
time: 482 us; the launch traced here: 479 us
  matrix products  270 us (56%)
  local copies, waits for them, and re-layouts  74.7 us (15%)
  blocking collectives  45.2 us (9%)
  waiting for transfers between devices  27.4 us (6%)
  other arithmetic  23.4 us (5%)
  starting transfers between devices  21.1 us (4%)
  between operations  16.8 us (3%)
    dot_general x27, matrix products, conv_taps(): jnp.dot(kernel[tap], window, preferred_element_type=jnp.float32)  152 us
    dot_general x27, matrix products, conv_back(): jnp.dot(kernel[tap].T, window, preferred_element_type=jnp.float32)  96.1 us
    psum x1, blocking collectives, body(): weight_grad = lax.psum(weight_local, 'dp') / (crop_rows * col_count)  37.7 us
    slice x2, local copies, waits for them, and re-layouts, conv_taps(): padded[:, tap_row:tap_row + out_rows, tap_col:tap_col + out_cols]  32.8 us
    slice x2, local copies, waits for them, and re-layouts, conv_back(): padded[:, 2 - tap_row:2 - tap_row + out_rows, 2 - tap_col:2 - tap_col + o...  32.1 us
    dot_general x9, matrix products, weight_taps(): parts.append(jnp.dot(window, flat.T, preferred_element_type=jnp.float32))  21.9 us
    reduce_scatter x1, waiting for transfers between devices, body(): eps = lax.psum_scatter(partial_value, 'mp', scatter_dimension=2, tiled=True)  19.7 us
    ppermute x4, starting transfers between devices, with_halo(): before = lax.ppermute(last, axis, up)  15.9 us
  transfers between devices with their start and end apart: 9, of which 5 were waited for; matrix products, arithmetic and copies ran while one was open for 0% of the time, Pallas kernels for 0%

commit v1 on v0

v1 whole, which is shorter than its diff:
```python
import functools

import jax
import jax.numpy as jnp
import numpy as np
from jax import lax
from jax.experimental import pallas as pl
from jax.experimental.pallas import tpu as pltpu
from jax.sharding import PartitionSpec as P

BLOCK = 16
HALO = 4
TILE = 4
PT_A = 0.5**0.5
PT_B = 2.0**0.5
STEPS = 1000
F32 = jnp.float32
BF16 = jnp.bfloat16


def dot(lhs, rhs, lhs_dim, rhs_dim):
    return lax.dot_general(
        lhs, rhs, (((lhs_dim,), (rhs_dim,)), ((), ())), preferred_element_type=F32
    )


def schedule_table():
    betas = np.linspace(0.00085**0.5, 0.012**0.5, STEPS, dtype=np.float32) ** 2
    table = np.cumprod(np.float32(1.0) - betas, dtype=np.float32)
    return np.pad(table, (0, 1024 - STEPS)).reshape(8, 128)


def roots(table_ref, step):
    rows = lax.broadcasted_iota(jnp.int32, (8, 128), 0)
    cols = lax.broadcasted_iota(jnp.int32, (8, 128), 1)
    hit = jnp.where(rows * 128 + cols == step, table_ref[...], 0.0)
    level = jnp.sum(jnp.sum(hit, axis=1, keepdims=True), axis=0, keepdims=True)
    return jnp.sqrt(level), jnp.sqrt(1.0 - level)


def band_tables(channels, lat):
    wide = BLOCK + 2
    tall = 3 * wide * lat
    picks = np.zeros((3, tall, 9 * lat), np.float32)
    for tap_row in range(3):
        for tap_col in range(3):
            for row in range(wide):
                for chan in range(lat):
                    spot = (tap_col * wide + row) * lat + chan
                    picks[tap_row, spot, (3 * tap_row + tap_col) * lat + chan] = 1.0
    spread = np.kron(np.eye(channels, dtype=np.float32), np.ones((1, BLOCK), np.float32))
    out_row = np.tile(np.repeat(np.arange(wide, dtype=np.int32), lat), 3)
    in_row = np.tile(np.arange(BLOCK, dtype=np.int32), channels)
    return picks, spread, out_row, in_row


def column_tables(cols):
    tiles = cols // TILE
    place = np.arange(cols)
    source = TILE * (place % tiles) + place // tiles
    gather = np.zeros((3, cols, cols), np.float32)
    scatter = np.zeros((3, cols, cols), np.float32)
    for tap_col in range(3):
        for spot in range(cols):
            taken = source[spot] + tap_col - 1
            if 0 <= taken < cols:
                gather[tap_col, taken, spot] = 1.0
                scatter[tap_col, spot, taken] = 1.0
    return gather, scatter.reshape(3 * cols, cols)


def eps_kernel(
    step_ref, me_ref, feat_ref, wout_ref, noisy_ref, table_ref, picks_ref, spread_ref,
    out_row_ref, in_row_ref, *refs, parts, rows, height, lat
):
    outs = refs[:parts]
    acc_ref, sum_ref, own_ref = refs[parts:]
    channels, cols = feat_ref.shape[0], feat_ref.shape[2]
    group = (BLOCK + 2) * lat
    gap = in_row_ref[...] - out_row_ref[...]
    band = jnp.zeros(gap.shape, F32)
    for tap_row in range(3):
        taps = dot(picks_ref[tap_row], wout_ref[...], 1, 1).astype(BF16)
        band = jnp.where(gap == tap_row - 2, dot(taps, spread_ref[...], 1, 0), band)
    band = band.astype(BF16)
    acc_ref[...] = jnp.zeros(acc_ref.shape, F32)
    for block in range(height // BLOCK):
        feats = feat_ref[:, block * BLOCK : (block + 1) * BLOCK, :]
        part = dot(band, feats.reshape(channels * BLOCK, cols), 1, 0)
        low = block * BLOCK * lat
        for tap_col in range(3):
            acc_ref[tap_col, low : low + group, :] += part[tap_col * group : (tap_col + 1) * group]
    spot = lax.broadcasted_iota(jnp.int32, (height * lat, cols), 1)
    inner = slice(lat, lat + height * lat)
    left = jnp.where(spot == 0, 0.0, pltpu.roll(acc_ref[0, inner, :], 1, 1))
    right = jnp.where(spot == cols - 1, 0.0, pltpu.roll(acc_ref[2, inner, :], cols - 1, 1))
    eps = left + acc_ref[1, inner, :] + right
    _, root_b = roots(table_ref, step_ref[0])
    edge = HALO * lat
    sum_ref[0:edge, :] = jnp.zeros((edge, cols), F32)
    sum_ref[edge + height * lat :, :] = jnp.zeros((edge, cols), F32)
    sum_ref[edge : edge + height * lat, :] = -root_b * eps
    for chan in range(lat):
        own_ref[pl.ds(chan, rows, stride=lat), :] = noisy_ref[0, chan]
    me = me_ref[0]
    low = pl.multiple_of(me * (rows * lat) + edge, 16)
    sum_ref[pl.ds(low, rows * lat), :] += own_ref[...]
    for part in range(parts):
        low = pl.multiple_of((me ^ part) * (rows * lat), 16)
        outs[part][...] = sum_ref[pl.ds(low, (rows + 2 * HALO) * lat), :].astype(BF16)


def prep_kernel(
    wmid_ref, wout_ref, picks_ref, spread_ref, out_row_ref, in_row_ref, planes_ref, band_ref
):
    for tap_row in range(3):
        first = wmid_ref[3 * tap_row].astype(F32)
        mid = wmid_ref[3 * tap_row + 1].astype(F32)
        last = wmid_ref[3 * tap_row + 2].astype(F32)
        even = (-2.0 / 3.0) * first + (-1.0 / 3.0) * last
        odd = (-2.0 / 3.0 * PT_A) * mid
        planes_ref[0, tap_row] = (even + odd).astype(BF16)
        planes_ref[1, tap_row] = (even - odd).astype(BF16)
        even = (1.0 / 6.0) * first + (1.0 / 3.0) * last
        odd = (1.0 / 6.0 * PT_B) * mid
        planes_ref[2, tap_row] = (even + odd).astype(BF16)
        planes_ref[3, tap_row] = (even - odd).astype(BF16)
    gap = in_row_ref[...] - out_row_ref[...]
    tall = dot(spread_ref[...], wout_ref[...], 0, 0).astype(BF16)
    band = jnp.zeros(gap.shape, F32)
    for tap_row in range(3):
        band = jnp.where(gap == tap_row - 2, dot(tall, picks_ref[tap_row], 1, 1), band)
    band_ref[...] = band.astype(BF16)


def to_planes(cells):
    tiles, chans = cells[0].shape
    none = jnp.zeros((1, chans), F32)
    d0 = jnp.concatenate([none, cells[3][: tiles - 1]], axis=0)
    d1, d2, d3, d4 = cells
    d5 = jnp.concatenate([cells[0][1:], none], axis=0)
    s1, s3 = PT_A * d1, PT_A * d3
    even_a, odd_a = d4 - 2.0 * d2, s3 - 2.0 * s1
    even_b, odd_b = d4 - 0.5 * d2, 2.0 * s3 - s1
    return (
        (d0 + d4) - 2.5 * d2,
        even_a + odd_a,
        even_a - odd_a,
        even_b + odd_b,
        even_b - odd_b,
        (d1 + d5) - 2.5 * d3,
    )


def from_planes(m0, ap, an, bp, bn, m5):
    sum_a, dif_a, sum_b, dif_b = ap + an, PT_A * (ap - an), bp + bn, PT_B * (bp - bn)
    return (
        m0 + sum_a + sum_b,
        dif_a + dif_b,
        0.5 * sum_a + 2.0 * sum_b,
        0.5 * dif_a + 2.0 * dif_b + m5,
    )


def from_planes_back(m0, ap, an, bp, bn, m5):
    sum_a, dif_a, sum_b, dif_b = ap + an, PT_A * (ap - an), bp + bn, PT_B * (bp - bn)
    return (
        m0 - 2.0 * sum_a - 0.5 * sum_b,
        -(2.0 * dif_a + 0.5 * dif_b),
        -(sum_a + sum_b),
        m5 - (dif_a + dif_b),
    )


def chunk_of(rows):
    return max(size for size in range(1, 19) if rows % size == 0)


def decoder_kernel(
    step_ref, me_ref, *refs, parts, rows, lat, cols
):
    blocks = refs[:parts]
    (table_ref, gather_ref, scatter_ref, win_ref, bin_ref, wback_ref, wmid_ref, planes_ref,
     bmid_ref, head_ref, out_ref, lat_ref, v1_ref, v2_ref, slope_ref, m_ref, hg_ref, x_ref,
     q_ref, lg_ref) = refs[parts:]
    tiles = cols // TILE
    me = me_ref[0]
    root_a, root_b = roots(table_ref, step_ref[0])
    total = blocks[0][...].astype(F32)
    for block in blocks[1:]:
        total = total + block[...].astype(F32)
    latent = (total / root_a).astype(BF16)
    lat_rows = (rows + 2 * HALO) * lat
    for tap_col in range(3):
        lat_ref[tap_col, 0:lat_rows, :] = dot(latent, gather_ref[tap_col], 1, 0)
        lat_ref[tap_col, lat_rows:, :] = jnp.zeros((8, cols), F32)

    hidden_rows, mixed_rows, grad_rows = rows + 6, rows + 4, rows + 2

    def hidden_step(pair, carry):
        wins = []
        for tap_col in range(3):
            low = pl.multiple_of(pair * 8, 8)
            rows24 = lat_ref[tap_col, pl.ds(low, 24), :]
            wins.append(jnp.concatenate([rows24[0:16], rows24[4:20]], axis=1))
        window = jnp.concatenate(wins, axis=0).astype(BF16)
        pre = dot(window, win_ref[...], 0, 0) + bin_ref[...]
        sig = 0.5 + 0.5 * jnp.tanh(0.5 * pre)
        act = pre * sig
        low = pl.multiple_of(pair * (2 * cols), 2 * cols)
        slope_ref[pl.ds(low, 2 * cols), :] = sig + act * (1.0 - sig)
        for half in range(2):
            cells = [
                act[half * cols + part * tiles : half * cols + (part + 1) * tiles]
                for part in range(TILE)
            ]
            low = pl.multiple_of((2 * pair + half) * tiles, tiles)
            for plane, value in enumerate(to_planes(cells)):
                v1_ref[plane, pl.ds(low, tiles), :] = value.astype(BF16)
        return carry

    lax.fori_loop(0, hidden_rows // 2, hidden_step, 0)

    def clear(ref, count, total_rows, width):
        @pl.when(me == 0)
        def _():
            for plane in range(ref.shape[0]):
                ref[plane, 0 : count * width, :] = jnp.zeros((count * width, ref.shape[2]), BF16)

        @pl.when(me == parts - 1)
        def _():
            for plane in range(ref.shape[0]):
                ref[plane, (total_rows - count) * width : total_rows * width, :] = jnp.zeros(
                    (count * width, ref.shape[2]), BF16
                )

    clear(v1_ref, 3, hidden_rows, tiles)

    chunk = chunk_of(mixed_rows)

    def mixed_chunk(index, carry):
        base = index * chunk
        for plane in range(6):
            value = None
            for tap_row in range(3):
                if plane == 0:
                    kern = wmid_ref[3 * tap_row]
                elif plane == 5:
                    kern = wmid_ref[3 * tap_row + 2]
                else:
                    kern = planes_ref[plane - 1, tap_row]
                low = pl.multiple_of((base + tap_row) * tiles, tiles)
                part = dot(v1_ref[plane, pl.ds(low, chunk * tiles), :], kern, 1, 1)
                value = part if value is None else value + part
            m_ref[plane, 0 : chunk * tiles, :] = value

        def mixed_step(row, inner):
            low = pl.multiple_of(row * tiles, tiles)
            cells = from_planes(*[m_ref[plane, pl.ds(low, tiles), :] for plane in range(6)])
            grads = []
            for cell in cells:
                pre = cell + bmid_ref[...]
                sig = 0.5 + 0.5 * jnp.tanh(0.5 * pre)
                grads.append(head_ref[...] * (sig * (1.0 + pre * (1.0 - sig))))
            low = pl.multiple_of((base + row) * tiles, tiles)
            for plane, value in enumerate(to_planes(grads)):
                v2_ref[plane, pl.ds(low, tiles), :] = value.astype(BF16)
            return inner

        lax.fori_loop(0, chunk, mixed_step, 0)
        return carry

    lax.fori_loop(0, mixed_rows // chunk, mixed_chunk, 0)
    clear(v2_ref, 2, mixed_rows, tiles)

    back = chunk_of(grad_rows)

    def grad_chunk(index, carry):
        base = index * back
        for plane in range(6):
            value = None
            for shift in range(3):
                tap_row = 2 - shift
                if plane == 0:
                    kern = wmid_ref[3 * tap_row + 2]
                elif plane == 5:
                    kern = wmid_ref[3 * tap_row]
                else:
                    kern = planes_ref[(plane - 1) ^ 2, tap_row]
                low = pl.multiple_of((base + shift) * tiles, tiles)
                part = dot(v2_ref[plane, pl.ds(low, back * tiles), :], kern, 1, 0)
                value = part if value is None else value + part
            m_ref[plane, 0 : back * tiles, :] = value

        def grad_step(row, inner):
            low = pl.multiple_of(row * tiles, tiles)
            cells = from_planes_back(*[m_ref[plane, pl.ds(low, tiles), :] for plane in range(6)])
            for part, cell in enumerate(cells):
                low = pl.multiple_of((base + row) * cols + part * tiles, tiles)
                slope_low = pl.multiple_of((base + row + 2) * cols + part * tiles, tiles)
                hg_ref[0, pl.ds(low, tiles), :] = (
                    cell * slope_ref[pl.ds(slope_low, tiles), :]
                ).astype(BF16)
            return inner

        lax.fori_loop(0, back, grad_step, 0)
        return carry

    lax.fori_loop(0, grad_rows // back, grad_chunk, 0)
    clear(hg_ref, 1, grad_rows, cols)

    taps = dot(wback_ref[...], hg_ref[0], 1, 1)
    for row in range(grad_rows):
        for tap_col in range(3):
            x_ref[16 * row : 16 * row + 16, tap_col * cols : (tap_col + 1) * cols] = taps[
                16 * tap_col : 16 * tap_col + 16, row * cols : (row + 1) * cols
            ]
    value = x_ref[...]
    high = value.astype(BF16)
    rest = (value - high.astype(F32)).astype(BF16)
    q_ref[...] = dot(high, scatter_ref[...], 1, 0) + dot(rest, scatter_ref[...], 1, 0)
    for row in range(rows):
        lg_ref[lat * row : lat * row + lat, :] = (
            q_ref[16 * (row + 2) : 16 * (row + 2) + lat, :]
            + q_ref[16 * (row + 1) + lat : 16 * (row + 1) + 2 * lat, :]
            + q_ref[16 * row + 2 * lat : 16 * row + 3 * lat, :]
        )
    out_ref[...] = (-(root_b / root_a) * lg_ref[...]).astype(BF16)


def fill_windows(noise_ref, win_ref, lat):
    tall, cols = noise_ref.shape
    noise = noise_ref[...].astype(F32)
    spot = lax.broadcasted_iota(jnp.int32, (tall, cols), 1)
    none = jnp.zeros((lat, cols), F32)
    moved = (
        jnp.where(spot == cols - 1, 0.0, pltpu.roll(noise, cols - 1, 1)),
        noise,
        jnp.where(spot == 0, 0.0, pltpu.roll(noise, 1, 1)),
    )
    for tap_col in range(3):
        win_ref[tap_col, 0:lat, :] = none
        win_ref[tap_col, lat : lat + tall, :] = moved[tap_col]
        win_ref[tap_col, lat + tall :, :] = none


def window_of(win_ref, block, lat):
    low = block * BLOCK * lat
    group = (BLOCK + 2) * lat
    return jnp.concatenate(
        [win_ref[tap_col, low : low + group, :] for tap_col in range(3)], axis=0
    ).astype(BF16)


def weight_kernel(
    feat_ref, noise_ref, picks_ref, out_row_ref, in_row_ref, out_ref, win_ref, *, lat
):
    channels, height, cols = feat_ref.shape
    fill_windows(noise_ref, win_ref, lat)
    total = None
    for block in range(height // BLOCK):
        feats = feat_ref[:, block * BLOCK : (block + 1) * BLOCK, :]
        part = dot(feats.reshape(channels * BLOCK, cols), window_of(win_ref, block, lat), 1, 1)
        total = part if total is None else total + part
    gap = in_row_ref[...] - out_row_ref[...]
    result = jnp.zeros(out_ref.shape, F32)
    for tap_row in range(3):
        kept = jnp.where(gap == tap_row - 2, total, 0.0)
        summed = jnp.sum(kept.reshape(channels, BLOCK, -1), axis=1)
        high = summed.astype(BF16)
        rest = summed - high.astype(F32)
        mid = rest.astype(BF16)
        low = (rest - mid.astype(F32)).astype(BF16)
        for piece in (high, mid, low):
            result = result + dot(piece, picks_ref[tap_row], 1, 0)
    out_ref[...] = result


def feature_kernel(band_ref, noise_ref, out_ref, win_ref, *, lat):
    channels, height, cols = out_ref.shape
    fill_windows(noise_ref, win_ref, lat)
    for block in range(height // BLOCK):
        value = dot(band_ref[...], window_of(win_ref, block, lat), 1, 0)
        out_ref[:, block * BLOCK : (block + 1) * BLOCK, :] = value.astype(BF16).reshape(
            channels, BLOCK, cols
        )


VMEM = pl.BlockSpec(memory_space=pltpu.VMEM)
SMEM = pl.BlockSpec(memory_space=pltpu.SMEM)
PARAMS = pltpu.CompilerParams(vmem_limit_bytes=60 * 2**20)


def call(kernel, scalars, operands, outs, scratch, name):
    return pl.pallas_call(
        kernel,
        in_specs=[SMEM] * len(scalars) + [VMEM] * len(operands),
        out_specs=jax.tree.map(lambda _: VMEM, outs),
        out_shape=outs,
        scratch_shapes=scratch,
        compiler_params=PARAMS,
        name=name,
    )(*scalars, *operands)


def body(features, w_out, noisy_latent, timestep, w_in, b_in, w_mid, b_mid, reward_head):
    _, channels, height, cols = features.shape
    lat, rows = noisy_latent.shape[1:3]
    chans = w_mid.shape[1]
    tiles = cols // TILE
    parts, images = lax.axis_size("mp"), lax.axis_size("dp")
    feats = features[0]
    me = lax.axis_index("mp").astype(jnp.int32).reshape(1)
    table = jnp.asarray(schedule_table())
    picks, spread, out_row, in_row = band_tables(channels, lat)
    picks, spread = jnp.asarray(picks, BF16), jnp.asarray(spread, BF16)
    gather, scatter = (jnp.asarray(part, BF16) for part in column_tables(cols))
    tall, deep = 3 * (BLOCK + 2) * lat, channels * BLOCK
    block_rows = (rows + 2 * HALO) * lat

    blocks = call(
        functools.partial(eps_kernel, parts=parts, rows=rows, height=height, lat=lat),
        (timestep, me),
        (feats, w_out, noisy_latent, table, picks, spread, out_row[:, None], in_row[None, :]),
        [jax.ShapeDtypeStruct((block_rows, cols), BF16) for _ in range(parts)],
        [
            pltpu.VMEM((3, (height + 2) * lat, cols), F32),
            pltpu.VMEM(((height + 2 * HALO) * lat, cols), F32),
            pltpu.VMEM((rows * lat, cols), F32),
        ],
        "eps_partial",
    )
    moved = [blocks[0]] + [
        lax.ppermute(blocks[part], "mp", [(i, i ^ part) for i in range(parts)])
        for part in range(1, parts)
    ]
    planes, band = call(
        prep_kernel,
        (),
        (w_mid, w_out, picks, spread, out_row[None, :], in_row[:, None]),
        [
            jax.ShapeDtypeStruct((4, 3, chans, chans), BF16),
            jax.ShapeDtypeStruct((deep, tall), BF16),
        ],
        [],
        "weight_planes",
    )
    taps = w_in.reshape(3, 3, chans, lat)
    win = jnp.pad(
        jnp.transpose(taps, (1, 0, 3, 2)).reshape(3, 3 * lat, chans), ((0, 0), (0, 16 - 3 * lat), (0, 0))
    ).reshape(48, chans)
    noise = call(
        functools.partial(decoder_kernel, parts=parts, rows=rows, lat=lat, cols=cols),
        (timestep, me),
        (*moved, table, gather, scatter, win, b_in[None, :], win, w_mid, planes, b_mid[None, :],
         reward_head[None, :]),
        jax.ShapeDtypeStruct((rows * lat, cols), BF16),
        [
            pltpu.VMEM((3, block_rows + 8, cols), F32),
            pltpu.VMEM((6, (rows + 6) * tiles, chans), BF16),
            pltpu.VMEM((6, (rows + 4) * tiles, chans), BF16),
            pltpu.VMEM(((rows + 6) * cols, chans), F32),
            pltpu.VMEM((6, max(chunk_of(rows + 4), chunk_of(rows + 2)) * tiles, chans), F32),
            pltpu.VMEM((1, (rows + 2) * cols, chans), BF16),
            pltpu.VMEM(((rows + 2) * 16, 3 * cols), F32),
            pltpu.VMEM(((rows + 2) * 16, cols), F32),
            pltpu.VMEM((rows * lat, cols), F32),
        ],
        "decoder",
    )
    full = lax.all_gather(noise, "mp", axis=0, tiled=True)
    weight_grad = call(
        functools.partial(weight_kernel, lat=lat),
        (),
        (feats, full, picks, out_row[None, :], in_row[:, None]),
        jax.ShapeDtypeStruct((channels, 9 * lat), F32),
        [pltpu.VMEM((3, (height + 2) * lat, cols), F32)],
        "weight_grad",
    )
    stage = 1
    while stage < images:
        weight_grad = weight_grad + lax.ppermute(
            weight_grad, "dp", [(i, i ^ stage) for i in range(images)]
        )
        stage *= 2
    feature_grads = call(
        functools.partial(feature_kernel, lat=lat),
        (),
        (band, full),
        jax.ShapeDtypeStruct((channels, height, cols), BF16),
        [pltpu.VMEM((3, (height + 2) * lat, cols), F32)],
        "feature_grads",
    )
    return feature_grads[None], weight_grad / (height * cols)


def solution(mesh):
    in_specs = (
        P("dp", "mp", None, None),
        P("mp", None),
        P("dp", None, "mp", None),
        P("dp"),
        P(),
        P(),
        P(),
        P(),
        P(),
    )
    out_specs = (P("dp", "mp", None, None), P("mp", None))
    return jax.shard_map(body, mesh=mesh, in_specs=in_specs, out_specs=out_specs, check_vma=False)
```

time: 482 us -> 100 us (0.21)
  matrix products: 270 us -> 0 us
  Pallas kernels: 0 us -> 72.3 us
  local copies, waits for them, and re-layouts: 74.7 us -> 4.13 us
  blocking collectives: 45.2 us -> 7.1 us
  other arithmetic: 23.4 us -> 0.8 us
  waiting for transfers between devices: 27.4 us -> 5.15 us
  between operations: 16.8 us -> 1.34 us
  starting transfers between devices: 21.1 us -> 8.78 us
    dot_general x63 -> x0, matrix products: 270 us -> none  [the longest x27 152 us: conv_taps(): jnp.dot(kernel[tap], window, preferred_element_type=jnp.float32)]
    pallas_call x0 -> x5, Pallas kernels: none -> 72.3 us  [call(): pl.pallas_call(kernel, in_specs=[SMEM] * len(scalars) + [VMEM] * len(oper...]
    slice x9 -> x0, local copies, waits for them, and re-layouts: 65 us -> none  [the longest x2 32.8 us: conv_taps(): padded[:, tap_row:tap_row + out_rows, tap_col:tap_col + out_cols]]
    psum x1 -> x0, blocking collectives: 37.7 us -> none  [body(): weight_grad = lax.psum(weight_local, 'dp') / (crop_rows * col_count)]
    reduce_scatter x1 -> x0, waiting for transfers between devices: 19.7 us -> none  [body(): eps = lax.psum_scatter(partial_value, 'mp', scatter_dimension=2, tiled=True)]
    convert_element_type x4 -> x0, other arithmetic: 18 us -> none  [the longest x1 7.38 us: body(): hidden_grad = (act_grad * slope(hidden_pre)).astype(jnp.bfloat16)]
    ppermute x8 -> x6, starting transfers between devices: 21 us -> 8.78 us  [the longest x3 5.67 us: body(): lax.ppermute(weight_grad, 'dp', [(i, i ^ stage) for i in range(images)])]
    unnamed x101 -> x8, local copies, waits for them, and re-layouts: 8.77 us -> 2.7 us
  transfers between devices with their start and end apart: 9 -> 6, of which waited for: 5 -> 2; matrix products, arithmetic and copies ran while one was open for 0% -> 1% of each run, Pallas kernels for 0% -> 14%
where the time goes in v1:
time: 100 us; the launch traced here: 99.6 us
  Pallas kernels  72.3 us (72%)
  starting transfers between devices  8.78 us (9%)
  blocking collectives  7.1 us (7%)
  waiting for transfers between devices  5.15 us (5%)
  local copies, waits for them, and re-layouts  4.13 us (4%)
  between operations  1.34 us (1%)
    pallas_call x5, Pallas kernels, call(): pl.pallas_call(kernel, in_specs=[SMEM] * len(scalars) + [VMEM] * len(oper...  72.3 us
    all_gather x1, blocking collectives, body(): full = lax.all_gather(noise, 'mp', axis=0, tiled=True)  7.1 us
    ppermute x3, starting transfers between devices, body(): lax.ppermute(weight_grad, 'dp', [(i, i ^ stage) for i in range(images)])  5.67 us
    ppermute x3, waiting for transfers between devices, body(): lax.ppermute(weight_grad, 'dp', [(i, i ^ stage) for i in range(images)])  5.14 us
    ppermute x3, starting transfers between devices, body(): lax.ppermute(blocks[part], 'mp', [(i, i ^ part) for i in range(parts)])  3.11 us
    unnamed x8, local copies, waits for them, and re-layouts  2.7 us
  transfers between devices with their start and end apart: 6, of which 2 were waited for; matrix products, arithmetic and copies ran while one was open for 1% of the time, Pallas kernels for 14%

profile of v1, /device:TPU:0, one launch (start us, length us, event | category | flops | bytes accessed | tf_op | source)
XLA Modules:
  0.0 99.6 jit_solution(10727707184122551982)
XLA Ops:
  1.3 1.4 %copy.22.wout_ref = bf16[80,36]{1,0:T(8,128)(2,1)} copy(bf16[80,36]{0,1:T(8,128)(2,1)} %param.21) | data formatting | bytes 11520 | tf_op args[1]
  2.7 4.9 %eps_partial.1 = (bf16[160,128]{1,0:T(8,128)(2,1)}, bf16[160,128]{1,0:T(8,128)(2,1)}, bf16[160,128]{1,0:T(8,128)(2,1)}, bf16[160,128]{1,0:T(8,128)(2,1)}) custom-call(s32[1]{0:T(128)S(6)} %copy.26.step_ref, s32[1]{0:T(128)} %bitcast.me_ref, bf16[80,128,128]{2,1,0:T(8,128)(2,1)} %bitcast.10, bf16[80,36]{1,0:T(8,128)(2,1)} %copy.22.wout_ref, ...), custom_call_target="tpu_custom_call" | custom-call | tf_op jit(solution)/shard_map/eps_partial/pallas_call | solution.py:395
  7.6 0.5 collective-permute-start
  8.1 2.6 %collective-permute-start.1 = (bf16[160,128]{1,0:T(8,128)(2,1)}, bf16[160,128]{1,0:T(8,128)(2,1)S(1)}, u32[]{:S(2)}, u32[]{:S(2)}) collective-permute-start(bf16[160,128]{1,0:T(8,128)(2,1)} %get-tuple-element.11), channel_id=1, source_target_pairs={{0,2},{1,3},{2,0},{3,1},{4,6},{5,7},{6,4},{7,5},{8,10},{9,11},{10,... | collective-permute-start | bytes 122888 | tf_op jit(solution)/shard_map/ppermute | solution.py:434
  10.6 0.1 collective-permute-start.2
  10.7 0.8 copy.24
  11.6 0.6 pad.4
  12.2 10.0 %weight_planes.1 = (bf16[4,3,512,512]{3,2,1,0:T(8,128)(2,1)}, bf16[1280,216]{1,0:T(8,128)(2,1)}) custom-call(bf16[9,512,512]{2,1,0:T(8,128)(2,1)} %refs_10_.1, bf16[80,36]{1,0:T(8,128)(2,1)} %copy.22.wout_ref, bf16[3,216,36]{2,1,0:T(8,128)(2,1)} %constant.29.clone.picks_ref, bf16[80,1280]{1,0:T(8,128)(2,1)} %constant.30.clone.spread_ref, ...), custom_call_target="tpu_custom_call" | custom-call | tf_op jit(solution)/shard_map/weight_planes/pallas_call | solution.py:395
  22.2 0.0 collective-permute-done.refs_1_
  22.2 0.0 copy-start
  22.2 0.0 collective-permute-done.1.refs_2_
  22.2 0.0 copy-start.1
  22.2 0.0 collective-permute-done.2.refs_3_
  22.3 0.0 copy-start.2
  22.3 0.6 copy-done
  22.8 0.0 copy-done.1
  22.9 0.0 copy-done.2
  22.9 47.2 %decoder.1 = bf16[128,128]{1,0:T(8,128)(2,1)} custom-call(s32[1]{0:T(128)S(6)} %copy.26.step_ref, s32[1]{0:T(128)} %bitcast.me_ref, bf16[160,128]{1,0:T(8,128)(2,1)} %get-tuple-element.9.refs_0_, bf16[160,128]{1,0:T(8,128)(2,1)} %copy-done, bf16[160,128]{1,0:T(8,128)(2,1)} %copy-done.1, bf16[160,128]{1,0:T(8,128)(2,1)} %copy-done.2, ...), custom_call_target="tpu_custom_call" | custom-call | tf_op jit(solution)/shard_map/decoder/pallas_call | solution.py:395
  70.1 7.1 %all_gather.3.noise_ref = bf16[512,128]{1,0:T(8,128)(2,1)} all-gather(bf16[128,128]{1,0:T(8,128)(2,1)} %decoder.1), channel_id=1, replica_groups=mesh['dp'=8,'mp'=4] {'mp'}, dimensions={0}, use_global_device_ids=true | all-gather | bytes 163840 | tf_op jit(solution)/shard_map/all_gather | solution.py:471
  77.2 6.0 %weight_grad.1 = f32[80,36]{1,0:T(8,128)} custom-call(bf16[80,128,128]{2,1,0:T(8,128)(2,1)} %bitcast.11, bf16[512,128]{1,0:T(8,128)(2,1)} %all_gather.3.noise_ref, bf16[3,216,36]{2,1,0:T(8,128)(2,1)} %constant.29.clone.picks_ref, s32[1,216]{1,0:T(1,128)} %constant.35.clone.out_row_ref, s32[1280,1]{1,0:T(8,128)} %constant.36.clone.in_row_ref), custom_call_target="tpu_custom_call" | custom-call | tf_op jit(solution)/shard_map/weight_grad/pallas_call | solution.py:395
  83.1 1.5 %collective-permute-start.3 = (f32[80,36]{1,0:T(8,128)}, f32[80,36]{1,0:T(8,128)S(1)}, u32[]{:S(2)}, u32[]{:S(2)}) collective-permute-start(f32[80,36]{1,0:T(8,128)} %weight_grad.1), channel_id=1, source_target_pairs={{0,4},{4,0},{8,12},{12,8},{16,20},{20,16},{24,28},{28,24},{1,5},{5... | collective-permute-start | bytes 34568 | tf_op jit(solution)/shard_map/ppermute | solution.py:482
  84.6 2.7 %collective-permute-done.3 = f32[80,36]{1,0:T(8,128)S(1)} collective-permute-done((f32[80,36]{1,0:T(8,128)}, f32[80,36]{1,0:T(8,128)S(1)}, u32[]{:S(2)}, u32[]{:S(2)}) %collective-permute-start.3) | collective-permute-done | bytes 11552 | tf_op jit(solution)/shard_map/ppermute | solution.py:482
  87.3 0.8 add.11
  88.1 1.6 %collective-permute-start.4 = (f32[80,36]{1,0:T(8,128)S(1)}, f32[80,36]{1,0:T(8,128)S(1)}, u32[]{:S(2)}, u32[]{:S(2)}) collective-permute-start(f32[80,36]{1,0:T(8,128)S(1)} %add.11), channel_id=1, source_target_pairs={{0,8},{4,12},{8,0},{12,4},{16,24},{20,28},{24,16},{28,20},{1,9},{5... | collective-permute-start | bytes 34568 | tf_op jit(solution)/shard_map/ppermute | solution.py:482
  89.7 2.4 %collective-permute-done.4 = f32[80,36]{1,0:T(8,128)S(1)} collective-permute-done((f32[80,36]{1,0:T(8,128)S(1)}, f32[80,36]{1,0:T(8,128)S(1)}, u32[]{:S(2)}, u32[]{:S(2)}) %collective-permute-start.4) | collective-permute-done | bytes 11552 | tf_op jit(solution)/shard_map/ppermute | solution.py:482
  92.1 2.6 %collective-permute-start.5 = (f32[80,36]{1,0:T(8,128)S(1)}, f32[80,36]{1,0:T(8,128)S(1)}, u32[]{:S(2)}, u32[]{:S(2)}) collective-permute-start(f32[80,36]{1,0:T(8,128)S(1)} %add.12), channel_id=1, source_target_pairs={{0,16},{4,20},{8,24},{12,28},{16,0},{20,4},{24,8},{28,12},{1,17},{... | collective-permute-start | bytes 34568 | tf_op jit(solution)/shard_map/ppermute | solution.py:482
  94.7 4.2 %feature_grads.1 = bf16[80,128,128]{2,1,0:T(8,128)(2,1)} custom-call(bf16[1280,216]{1,0:T(8,128)(2,1)} %get-tuple-element.8.band_ref, bf16[512,128]{1,0:T(8,128)(2,1)} %all_gather.3.noise_ref), custom_call_target="tpu_custom_call" | custom-call | tf_op jit(solution)/shard_map/feature_grads/pallas_call | solution.py:395
  98.9 0.0 collective-permute-done.5
  98.9 0.7 copy.25
  (3 shorter events, 0.0 us)
Async XLA Ops:
  7.6 14.6 %collective-permute-start = (bf16[160,128]{1,0:T(8,128)(2,1)}, bf16[160,128]{1,0:T(8,128)(2,1)S(1)}, u32[]{:S(2)}, u32[]{:S(2)}) collective-permute-start(bf16[160,128]{1,0:T(8,128)(2,1)} %get-tuple-element.10), channel_id=1, source_target_pairs={{0,1},{1,0},{2,3},{3,2},{4,5},{5,4},{6,7},{7,6},{8,9},{9,8},{10,11... | collective-permute-start | bytes 122888 | tf_op jit(solution)/shard_map/ppermute | solution.py:434
  8.1 14.1 %collective-permute-start.1 = (bf16[160,128]{1,0:T(8,128)(2,1)}, bf16[160,128]{1,0:T(8,128)(2,1)S(1)}, u32[]{:S(2)}, u32[]{:S(2)}) collective-permute-start(bf16[160,128]{1,0:T(8,128)(2,1)} %get-tuple-element.11), channel_id=1, source_target_pairs={{0,2},{1,3},{2,0},{3,1},{4,6},{5,7},{6,4},{7,5},{8,10},{9,11},{10,... | collective-permute-start | bytes 122888 | tf_op jit(solution)/shard_map/ppermute | solution.py:434
  10.6 11.6 %collective-permute-start.2 = (bf16[160,128]{1,0:T(8,128)(2,1)}, bf16[160,128]{1,0:T(8,128)(2,1)S(1)}, u32[]{:S(2)}, u32[]{:S(2)}) collective-permute-start(bf16[160,128]{1,0:T(8,128)(2,1)} %get-tuple-element.12), channel_id=1, source_target_pairs={{0,3},{1,2},{2,1},{3,0},{4,7},{5,6},{6,5},{7,4},{8,11},{9,10},{10,... | collective-permute-start | bytes 122888 | tf_op jit(solution)/shard_map/ppermute | solution.py:434
  22.2 0.6 copy-start
  22.2 0.6 copy-start.1
  22.3 0.6 copy-start.2
  83.1 4.2 %collective-permute-start.3 = (f32[80,36]{1,0:T(8,128)}, f32[80,36]{1,0:T(8,128)S(1)}, u32[]{:S(2)}, u32[]{:S(2)}) collective-permute-start(f32[80,36]{1,0:T(8,128)} %weight_grad.1), channel_id=1, source_target_pairs={{0,4},{4,0},{8,12},{12,8},{16,20},{20,16},{24,28},{28,24},{1,5},{5... | collective-permute-start | bytes 34568 | tf_op jit(solution)/shard_map/ppermute | solution.py:482
  88.1 4.0 %collective-permute-start.4 = (f32[80,36]{1,0:T(8,128)S(1)}, f32[80,36]{1,0:T(8,128)S(1)}, u32[]{:S(2)}, u32[]{:S(2)}) collective-permute-start(f32[80,36]{1,0:T(8,128)S(1)} %add.11), channel_id=1, source_target_pairs={{0,8},{4,12},{8,0},{12,4},{16,24},{20,28},{24,16},{28,20},{1,9},{5... | collective-permute-start | bytes 34568 | tf_op jit(solution)/shard_map/ppermute | solution.py:482
  92.1 6.8 %collective-permute-start.5 = (f32[80,36]{1,0:T(8,128)S(1)}, f32[80,36]{1,0:T(8,128)S(1)}, u32[]{:S(2)}, u32[]{:S(2)}) collective-permute-start(f32[80,36]{1,0:T(8,128)S(1)} %add.12), channel_id=1, source_target_pairs={{0,16},{4,20},{8,24},{12,28},{16,0},{20,4},{24,8},{28,12},{1,17},{... | collective-permute-start | bytes 34568 | tf_op jit(solution)/shard_map/ppermute | solution.py:482
